TPU v7x, 768 devices: a whole 4x8x12 slice. The times are simulated.
768 devices in a mesh: ein: 32 (over y, x_lo, core), eout: 24 (over z, x_hi).
Axes of the slice: x: 4 (x_hi: 2, x_lo: 2; x = x_hi * 2 + x_lo), y: 8, z: 12, core: 2. Of those that a mesh axis runs over, the one named last changes fastest.
Arguments:
- activations: bfloat16 [768, 28672], P('eout', 'ein'), may hold values from -6 to 6
- gradients: bfloat16 [768, 8192], P('eout'), may hold values from -6 to 6
- eigvec_in: bfloat16 [28672, 24576], P('ein', 'eout'), may hold values from -0.03125 to 0.03125
- eigvec_out: bfloat16 [8192, 8192], P(None, 'ein'), may hold values from -0.0625 to 0.0625
- lengths: int32 [2], replicated, may hold values from 96 to 384
Outputs:
- correction: float32 [24576, 8192], P('eout', 'ein')
All inputs are finite; a program needn't handle non-finite values.
Results may differ from a plain program's by a relative error of at most 0.0044.
Values may be sent and summed in bfloat16 or wider, within the bound.
A program may use at most 32 MiB of HBM per device.

v0:
```python
import jax
import jax.numpy as jnp
from jax import lax
from jax.sharding import PartitionSpec as P

LEN = 384
DOCS = 2


def body(activations, gradients, eigvec_in, eigvec_out, lengths):
    rows_grad = gradients.shape[0]
    grad_start = lax.axis_index("eout") * rows_grad
    positions = grad_start + jnp.arange(rows_grad, dtype=jnp.int32)
    doc_index = positions // LEN
    matches = doc_index[:, None] == jnp.arange(DOCS, dtype=jnp.int32)[None, :]
    limits = jnp.sum(jnp.where(matches, lengths[None, :], 0), axis=1)
    kept = positions % LEN < limits
    grad_product = jnp.dot(gradients, eigvec_out, preferred_element_type=jnp.float32)
    grad_local = jnp.where(kept[:, None], grad_product, 0.0).astype(jnp.bfloat16)
    rotated_grad = lax.all_gather(grad_local, "eout", axis=0, tiled=True)
    partial_act = jnp.dot(
        lax.all_gather(activations, "eout", axis=0, tiled=True),
        eigvec_in,
        preferred_element_type=jnp.float32,
    )
    act_part = lax.psum_scatter(partial_act, "ein", scatter_dimension=0, tiled=True).astype(
        jnp.bfloat16
    )
    rotated_act = lax.all_gather(act_part, "ein", axis=0, tiled=True)
    act_docs = rotated_act.reshape(DOCS, LEN, -1)
    grad_docs = rotated_grad.reshape(DOCS, LEN, -1)
    rotated = jnp.einsum("dtk,dtg->dkg", act_docs, grad_docs, preferred_element_type=jnp.float32)
    denominator = jnp.sum(lengths).astype(jnp.float32)
    return jnp.sum(rotated * rotated, axis=0) / denominator


def solution(mesh):
    in_specs = (P("eout", "ein"), P("eout", None), P("ein", "eout"), P(None, "ein"), P())
    out_specs = P("eout", "ein")
    return jax.shard_map(body, mesh=mesh, in_specs=in_specs, out_specs=out_specs, check_vma=False)
```

profile of v0, /device:TPU:1, one launch (start us, length us, event | category | flops | bytes accessed | tf_op | source)
XLA Modules:
  0.0 347.3 jit_solution(11726211120648790928)
XLA Ops:
  6.5 0.0 copy-start
  6.5 0.0 all-gather.3.cloned.1.call-start
  6.5 0.7 all-gather.3.cloned.1.call-update
  7.3 0.0 reduce-scatter.2.cloned.1.call-start
  7.3 125.7 %all-gather.3.cloned.1.call-done = bf16[768,896]{1,0:T(8,128)(2,1)} async-done(((bf16[32,896]{1,0:T(8,128)(2,1)}), bf16[768,896]{1,0:T(8,128)(2,1)}) %all-gather.3.cloned.1.call-update) | async-done | bytes 1376272 | tf_op jit(solution)/shard_map/all_gather | solution.py:22
  133.0 0.0 copy-done
  133.0 4.8 %fusion.4 = f32[768,1024]{1,0:T(8,128)} fusion(bf16[768,896]{1,0:T(8,128)(2,1)} %all-gather.3.cloned.1.call-done, bf16[896,1024]{1,0:T(8,128)(2,1)S(1)} %copy-done), kind=kOutput, calls=%fused_computation.11 | convolution fusion | flops 1409286144 | bytes 6356992 | tf_op jit(solution)/shard_map/dot_general | solution.py:21
  137.8 0.0 copy-start.2
  137.8 0.0 copy-start.1
  137.8 0.0 reduce-scatter.2.cloned.1.call-update
  137.9 0.0 all-gather.5.cloned.1.call-start
  137.9 126.3 %reduce-scatter.2.cloned.1.call-done = f32[24,1024]{1,0:T(8,128)} async-done(((f32[768,1024]{1,0:T(8,128)}), f32[24,1024]{1,0:T(8,128)}) %reduce-scatter.2.cloned.1.call-update) | async-done | bytes 98320 | tf_op jit(solution)/shard_map/reduce_scatter | solution.py:26
  264.2 1.5 convert_element_type.9
  265.8 0.0 all-gather.5.cloned.1.call-update
  265.8 0.0 copy-done.2
  265.8 0.7 reduce_sum.29
  267.2 0.1 fusion.1
  267.3 0.0 copy-done.1
  267.3 3.0 fusion
  270.3 50.1 %all_gather.11 = bf16[768,256]{1,0:T(8,128)(2,1)S(1)} all-gather(bf16[32,256]{1,0:T(8,128)(2,1)S(1)} %fusion), channel_id=1, replica_groups=mesh['ein'=32,'eout'=24] {'eout'}, dimensions={0}, use_global_device_ids=true | all-gather | bytes 409600 | tf_op jit(solution)/shard_map/all_gather | solution.py:20
  320.4 17.0 %all-gather.5.cloned.1.call-done = bf16[768,1024]{1,0:T(8,128)(2,1)} async-done(((bf16[24,1024]{1,0:T(8,128)(2,1)}), bf16[768,1024]{1,0:T(8,128)(2,1)}) %all-gather.5.cloned.1.call-update) | async-done | bytes 1572880 | tf_op jit(solution)/shard_map/all_gather | solution.py:29
  337.4 2.3 multiply_reduce_fusion
  339.7 1.0 broadcast_divide_fusion
  (2 shorter events, 0.0 us)
Async XLA Ops:
  6.5 126.5 %copy-start = (bf16[896,1024]{1,0:T(8,128)(2,1)S(1)}, bf16[896,1024]{1,0:T(8,128)(2,1)}, u32[]{:S(2)}) copy-start(bf16[896,1024]{1,0:T(8,128)(2,1)} %param.7) | copy-start | bytes 5505028
  6.5 126.5 %all-gather.3.cloned.1.call-start = ((), (), s32[]{:S(2)}) async-start(), calls=%async_computation.1 | async-start | bytes 1433600 | tf_op jit(solution)/shard_map/all_gather | solution.py:22
  7.3 257.0 %reduce-scatter.2.cloned.1.call-start = ((), (), s32[]{:S(2)}) async-start(), calls=%async_computation.2 | async-start | bytes 3244032 | tf_op jit(solution)/shard_map/reduce_scatter | solution.py:26
  137.8 128.0 %copy-start.2 = (s32[2]{0:T(128)S(1)}, s32[2]{0:T(128)}, u32[]{:S(2)}) copy-start(s32[2]{0:T(128)} %param.9) | copy-start | bytes 28
  137.8 129.4 %copy-start.1 = (bf16[32,8192]{1,0:T(8,128)(2,1)S(1)}, bf16[32,8192]{1,0:T(8,128)(2,1)}, u32[]{:S(2)}) copy-start(bf16[32,8192]{1,0:T(8,128)(2,1)} %param.6) | copy-start | bytes 1572868
  137.9 199.6 %all-gather.5.cloned.1.call-start = ((), (), s32[]{:S(2)}) async-start(), calls=%async_computation.3 | async-start | bytes 1622016 | tf_op jit(solution)/shard_map/all_gather | solution.py:29
Sparse Core Ops, SparseCore 0:
  10.9 122.0 all-gather.2
  138.0 126.2 reduce-scatter.1
  267.0 70.4 all-gather.4
where the time goes:
time: 348 us; the launch traced here: 347 us
  waiting for transfers between devices  270 us (78%)
  blocking collectives  50.1 us (14%)
  between operations  13.8 us (4%)
  matrix products  10.1 us (3%)
    reduce_scatter x1, waiting for transfers between devices, body(): lax.psum_scatter(partial_act, 'ein', scatter_dimension=0, tiled=True)  126 us
    all_gather x1, waiting for transfers between devices, body(): lax.all_gather(activations, 'eout', axis=0, tiled=True)  126 us
    all_gather x1, blocking collectives, body(): rotated_grad = lax.all_gather(grad_local, 'eout', axis=0, tiled=True)  50.1 us
    all_gather x1, waiting for transfers between devices, body(): rotated_act = lax.all_gather(act_part, 'ein', axis=0, tiled=True)  17 us
  transfers between devices with their start and end apart: 3, of which 3 were waited for; matrix products, arithmetic and copies ran while one was open for 1% of the time, Pallas kernels for 0%

commit v1 on v0

v1 whole, which is shorter than its diff:
```python
import jax
import jax.numpy as jnp
from jax import lax
from jax.experimental import pallas as pl
from jax.experimental.pallas import tpu as pltpu
from jax.sharding import PartitionSpec as P

LEN = 384
MESH = pl.DeviceIdType.MESH
F32 = jnp.float32
BF16 = jnp.bfloat16

NZ = 12
NY = 8
SIZES = (192, 256, 256, 64)
OFFS = (0, 192, 448, 704)
SLOT = 64
HALF = 32


def up(k):
    return 0 if k == 0 else 2 * k - 1


def down(k):
    return 2 * k if k < 6 else 11


def kernel(
    act_in, grad_in, wi_in, wo_in, lengths, out,
    act, grads, wi, wo, gall, gdoc, part, core_r, x_s, x_r, y_s, y_r, full,
    local_sem, z_ss, z_rs, g_ss, g_rs, r_ss, r_rs,
):
    ein = lax.axis_index("ein")
    eout = lax.axis_index("eout")
    core = lax.rem(ein, 2)
    x_lo = lax.rem(lax.div(ein, 2), 2)
    y = lax.div(ein, 4)
    x_hi = lax.rem(eout, 2)
    z = lax.div(eout, 2)

    z_up = (ein, lax.rem(z + 1, NZ) * 2 + x_hi)
    z_dn = (ein, lax.rem(z + NZ - 1, NZ) * 2 + x_hi)
    hi_peer = (ein, z * 2 + 1 - x_hi)
    core_peer = (ein + 1 - 2 * core, eout)
    x_peer = (ein + 2 - 4 * x_lo, eout)
    y_of = [lax.rem(y + d, NY) for d in range(NY)]
    y_peer = [(y_of[d] * 4 + x_lo * 2 + core, eout) for d in range(NY)]

    act_copy = pltpu.make_async_copy(act_in, act.at[pl.ds(0, HALF)], local_sem.at[0])
    act_copy.start()
    grad_copy = pltpu.make_async_copy(grad_in, grads, local_sem.at[1])
    grad_copy.start()
    wo_copies = []
    for i in range(4):
        rows = pl.ds(i * 2048, 2048)
        wo_copies.append(pltpu.make_async_copy(wo_in.at[rows], wo.at[rows], local_sem.at[2 + i]))
        wo_copies[-1].start()
    wi_copy = pltpu.make_async_copy(wi_in, wi, local_sem.at[6])
    wi_copy.start()

    barrier = pltpu.get_barrier_semaphore()
    partners = [z_up, z_dn, hi_peer, core_peer, x_peer] + y_peer[1:]
    for peer in partners:
        pl.semaphore_signal(barrier, inc=1, device_id=peer, device_id_type=MESH)
    pl.semaphore_wait(barrier, len(partners))

    started = []

    def send(src, dst, ss, rs, peer):
        copy = pltpu.make_async_remote_copy(
            src_ref=src, dst_ref=dst, send_sem=ss, recv_sem=rs,
            device_id=peer, device_id_type=MESH,
        )
        copy.start()
        started.append(copy)
        return copy

    z_in = {}

    def act_unit(slot, h):
        return act.at[pl.ds(slot * SLOT + h * HALF, HALF)]

    def z_send(k, h):
        if k < 6 and not (k == 5 and h == 1):
            i = (k * 2 + h) * 2
            z_in["u", k + 1, h] = send(
                act_unit(up(k), h), act_unit(up(k + 1) if k < 5 else 11, h),
                z_ss.at[i], z_rs.at[i], z_dn)
        if k < 6 and not (k == 5 and h == 0):
            i = (k * 2 + h) * 2 + 1
            z_in["d", k + 1, h] = send(
                act_unit(down(k), h), act_unit(down(k + 1), h),
                z_ss.at[i], z_rs.at[i], z_up)

    def z_serve(k, h):
        if k == 0:
            hi_act.wait_recv()
            z_send(0, 1)
            return
        for way in "ud":
            if (way, k, h) in z_in:
                z_in[way, k, h].wait_recv()
        if k < 6:
            z_send(k, h)

    g_in = {}

    def g_rows(slot, h=None):
        if h is None:
            return gall.at[pl.ds(slot * SLOT, SLOT)]
        return gall.at[pl.ds(slot * SLOT + h * HALF, HALF)]

    def g_serve(k):
        if k == 0:
            hi_grad.wait_recv()
        else:
            for way in "ud":
                g_in[way, k].wait_recv()
        if k < 5:
            g_in["u", k + 1] = send(g_rows(up(k)), g_rows(up(k + 1)), g_ss.at[2 * k], g_rs.at[2 * k], z_dn)
            g_in["d", k + 1] = send(g_rows(down(k)), g_rows(down(k + 1)), g_ss.at[2 * k + 1], g_rs.at[2 * k + 1], z_up)
        elif k == 5:
            g_in["u", 6] = send(g_rows(up(5), 0), g_rows(11, 0), g_ss.at[10], g_rs.at[10], z_dn)
            g_in["d", 6] = send(g_rows(down(5), 1), g_rows(11, 1), g_ss.at[11], g_rs.at[11], z_up)

    def grad_part(first, count, total):
        def step(i, acc):
            at = pl.multiple_of(i * 1024, 1024)
            return acc + jnp.dot(
                grads[:, pl.ds(at, 1024)], wo[pl.ds(at, 1024), :], preferred_element_type=F32)
        return lax.fori_loop(first, first + count, step, total)

    def grad_done(total):
        limit = jnp.where(z < NZ // 2, lengths[0], lengths[1])
        start = lax.rem(z, NZ // 2) * SLOT + x_hi * HALF
        position = start + lax.broadcasted_iota(jnp.int32, (HALF, 256), 0)
        gall[pl.ds(0, HALF), :] = jnp.where(position < limit, total, 0.0).astype(BF16)

    red = {}

    def off2(g):
        return OFFS[g] // 2

    def off4(g):
        return OFFS[g] // 4

    def quarter(g, c, x):
        n = SIZES[g] // 4
        return pl.ds(pl.multiple_of(OFFS[g] + (c * 2 + x) * n, 16), n)

    def sem(g, i):
        return r_ss.at[g * 19 + i], r_rs.at[g * 19 + i]

    def gemm(g):
        rows = pl.ds(OFFS[g], SIZES[g])

        def step(c, carry):
            cols = pl.ds(pl.multiple_of(c * 256, 256), 256)
            product = jnp.dot(act[rows, :], wi[:, cols], preferred_element_type=F32)
            part[2 * c, rows, :] = product[:, :128]
            part[2 * c + 1, rows, :] = product[:, 128:]
            return carry

        lax.fori_loop(0, 4, step, 0)
        n = SIZES[g] // 2
        theirs = pl.ds(pl.multiple_of(OFFS[g] + (1 - core) * n, 16), n)
        red["c", g] = send(part.at[:, theirs], core_r.at[:, pl.ds(off2(g), n)], *sem(g, 0), core_peer)

    def in_half(g, x):
        n = SIZES[g] // 4
        return pl.ds(pl.multiple_of(off2(g) + x * n, 16), n)

    def stage_c(g):
        red["c", g].wait_recv()
        n = SIZES[g] // 4
        mine, got = quarter(g, core, 1 - x_lo), in_half(g, 1 - x_lo)

        def step(b, carry):
            x_s[b, pl.ds(off4(g), n), :] = (part[b, mine, :] + core_r[b, got, :]).astype(BF16)
            return carry

        lax.fori_loop(0, NY, step, 0)
        rows = pl.ds(off4(g), n)
        red["x", g] = send(x_s.at[:, rows], x_r.at[:, rows], *sem(g, 1), x_peer)

    def chip_pair_sum(g, b):
        n = SIZES[g] // 4
        return (part[b, quarter(g, core, x_lo), :] + core_r[b, in_half(g, x_lo), :]
                + x_r[b, pl.ds(off4(g), n), :].astype(F32))

    def stage_x(g):
        red["x", g].wait_recv()
        n = SIZES[g] // 4
        rows = pl.ds(off4(g), n)

        def step(b, carry):
            y_s[b, rows, :] = chip_pair_sum(g, b).astype(BF16)
            return carry

        lax.fori_loop(0, NY, step, 0)
        for d in (4, 3, 5, 2, 6, 1, 7):
            red["y", g, d] = send(
                y_s.at[y_of[d], rows], y_r.at[d - 1, rows], *sem(g, 1 + d), y_peer[d])

    def stage_y(g):
        n = SIZES[g] // 4
        rows = pl.ds(off4(g), n)
        total = chip_pair_sum(g, y)
        for d in range(1, NY):
            red["y", g, d].wait_recv()
        for d in range(1, NY):
            total = total + y_r[d - 1, rows, :].astype(F32)
        mine = quarter(g, core, x_lo)
        full[y, mine, :] = total.astype(BF16)
        for d in (4, 3, 5, 2, 6, 1, 7):
            red["f", g, d] = send(
                full.at[y, mine], full.at[y, mine], *sem(g, 8 + d), y_peer[d])

    def stage_f(g):
        mine = quarter(g, core, x_lo)
        for d in range(1, NY):
            recv = pltpu.make_async_remote_copy(
                src_ref=full.at[y, mine], dst_ref=full.at[y_of[NY - d], mine],
                send_sem=sem(g, 8 + d)[0], recv_sem=sem(g, 8 + d)[1],
                device_id=y_peer[d], device_id_type=MESH)
            recv.wait_recv()
        red["fx", g] = send(full.at[:, mine], full.at[:, mine], *sem(g, 16), x_peer)
        red["fc", g] = send(full.at[:, mine], full.at[:, mine], *sem(g, 17), core_peer)

    def wait_at(g, i, c, x, peer):
        rows = quarter(g, c, x)
        pltpu.make_async_remote_copy(
            src_ref=full.at[:, rows], dst_ref=full.at[:, rows],
            send_sem=sem(g, i)[0], recv_sem=sem(g, i)[1],
            device_id=peer, device_id_type=MESH).wait_recv()

    def stage_fx(g):
        wait_at(g, 16, core, 1 - x_lo, x_peer)
        theirs = quarter(g, core, 1 - x_lo)
        red["fxc", g] = send(full.at[:, theirs], full.at[:, theirs], *sem(g, 18), core_peer)

    def stage_fc(g):
        wait_at(g, 17, 1 - core, x_lo, core_peer)
        wait_at(g, 18, 1 - core, 1 - x_lo, core_peer)

    act_copy.wait()
    z_send(0, 0)
    hi_act = send(act_unit(0, 0), act_unit(0, 1), z_ss.at[24], z_rs.at[24], hi_peer)
    grad_copy.wait()
    for copy in wo_copies[:2]:
        copy.wait()
    total = grad_part(0, 4, jnp.zeros((HALF, 256), F32))
    z_serve(0, 1)
    for copy in wo_copies[2:]:
        copy.wait()
    grad_done(grad_part(4, 4, total))
    hi_grad = send(g_rows(0, 0), g_rows(0, 1), g_ss.at[12], g_rs.at[12], hi_peer)
    z_serve(1, 0)
    wi_copy.wait()
    z_serve(1, 1)
    gemm(0)
    z_serve(2, 0)
    g_serve(0)
    z_serve(2, 1)
    stage_c(0)
    z_serve(3, 0)
    g_serve(1)
    z_serve(3, 1)
    gemm(1)
    stage_x(0)
    z_serve(4, 0)
    stage_c(1)
    g_serve(2)
    z_serve(4, 1)
    stage_y(0)
    z_serve(5, 0)
    stage_x(1)
    g_serve(3)
    z_serve(5, 1)
    gemm(2)
    g_serve(4)
    stage_f(0)
    z_serve(6, 0)
    z_serve(6, 1)
    gemm(3)
    stage_c(2)
    stage_c(3)
    stage_y(1)
    stage_fx(0)
    g_serve(5)
    stage_x(2)
    stage_x(3)
    stage_f(1)
    g_serve(6)

    for slot in range(NZ):
        k = (slot + 1) // 2
        shift = k if slot % 2 else NZ - k
        doc = lax.div(lax.rem(z + shift, NZ), NZ // 2)
        rows = pl.ds(slot * SLOT, SLOT)
        values = gall[rows, :]
        zero = jnp.zeros_like(values)
        gdoc[rows, 0:256] = jnp.where(doc == 0, values, zero)
        gdoc[rows, 256:512] = jnp.where(doc == 1, values, zero)

    stage_fx(1)
    stage_y(2)
    stage_y(3)
    stage_f(2)
    stage_f(3)
    stage_fx(2)
    stage_fx(3)
    for g in range(4):
        stage_fc(g)

    denominator = (lengths[0] + lengths[1]).astype(F32)

    def outer(b, carry):
        both = lax.dot_general(
            full[b], gdoc[...], (((0,), (0,)), ((), ())), preferred_element_type=F32)
        squares = both[:, :256] * both[:, :256] + both[:, 256:] * both[:, 256:]
        out[pl.ds(pl.multiple_of(b * 128, 128), 128), :] = squares / denominator
        return carry

    lax.fori_loop(0, NY, outer, 0)

    for copy in started:
        copy.wait_send()


def body(activations, gradients, eigvec_in, eigvec_out, lengths):
    anywhere = pl.BlockSpec(memory_space=pl.ANY)
    dma = pltpu.SemaphoreType.DMA
    return pl.pallas_call(
        kernel,
        out_shape=jax.ShapeDtypeStruct((1024, 256), F32),
        in_specs=[anywhere] * 4 + [pl.BlockSpec(memory_space=pltpu.SMEM)],
        out_specs=pl.BlockSpec(memory_space=pltpu.VMEM),
        scratch_shapes=[
            pltpu.VMEM((768, 896), BF16),
            pltpu.VMEM((32, 8192), BF16),
            pltpu.VMEM((896, 1024), BF16),
            pltpu.VMEM((8192, 256), BF16),
            pltpu.VMEM((768, 256), BF16),
            pltpu.VMEM((768, 512), BF16),
            pltpu.VMEM((8, 768, 128), F32),
            pltpu.VMEM((8, 384, 128), F32),
            pltpu.VMEM((8, 192, 128), BF16),
            pltpu.VMEM((8, 192, 128), BF16),
            pltpu.VMEM((8, 192, 128), BF16),
            pltpu.VMEM((7, 192, 128), BF16),
            pltpu.VMEM((8, 768, 128), BF16),
            dma((7,)),
            dma((25,)),
            dma((25,)),
            dma((13,)),
            dma((13,)),
            dma((76,)),
            dma((76,)),
        ],
        compiler_params=pltpu.CompilerParams(
            collective_id=0, has_side_effects=True, vmem_limit_bytes=40 * 1024 * 1024),
        cost_estimate=pl.CostEstimate(
            flops=2_300_000_000, bytes_accessed=8_000_000, transcendentals=0),
    )(activations, gradients, eigvec_in, eigvec_out, lengths)


def solution(mesh):
    in_specs = (P("eout", "ein"), P("eout", None), P("ein", "eout"), P(None, "ein"), P())
    out_specs = P("eout", "ein")
    return jax.shard_map(body, mesh=mesh, in_specs=in_specs, out_specs=out_specs, check_vma=False)
```

time: 348 us -> 83.6 us (0.24)
  waiting for transfers between devices: 270 us -> 0 us
  Pallas kernels: 0 us -> 76.1 us
  blocking collectives: 50.1 us -> 0 us
  between operations: 13.8 us -> 0.01 us
  matrix products: 10.1 us -> 0 us
  local copies, waits for them, and re-layouts: 0.01 us -> 7.17 us
    all_gather x2 -> x0, waiting for transfers between devices: 143 us -> none  [the longest x1 126 us: body(): lax.all_gather(activations, 'eout', axis=0, tiled=True)]
    reduce_scatter x1 -> x0, waiting for transfers between devices: 126 us -> none  [body(): lax.psum_scatter(partial_act, 'ein', scatter_dimension=0, tiled=True)]
    pallas_call x0 -> x1, Pallas kernels: none -> 76.1 us  [body(): pl.pallas_call(kernel, out_shape=jax.ShapeDtypeStruct((1024, 256), F32),...]
    all_gather x1 -> x0, blocking collectives: 50.1 us -> none  [body(): rotated_grad = lax.all_gather(grad_local, 'eout', axis=0, tiled=True)]
    dot_general x3 -> x0, matrix products: 10.1 us -> none  [the longest x1 4.79 us: body(): jnp.dot(lax.all_gather(activations, 'eout', axis=0, tiled=True), eigvec_i...]
    unnamed x6 -> x11, local copies, waits for them, and re-layouts: 0.01 us -> 7.17 us
  transfers between devices with their start and end apart: 3 -> 0, of which waited for: 3 -> 0; matrix products, arithmetic and copies ran while one was open for 1% -> 0% of each run, Pallas kernels for 0% -> 0%
where the time goes in v1:
time: 83.6 us; the launch traced here: 83.3 us
  Pallas kernels  76.1 us (91%)
  local copies, waits for them, and re-layouts  7.17 us (9%)
    pallas_call x1, Pallas kernels, body(): pl.pallas_call(kernel, out_shape=jax.ShapeDtypeStruct((1024, 256), F32),...  76.1 us
    unnamed x11, local copies, waits for them, and re-layouts  7.17 us

profile of v1, /device:TPU:1, one launch (start us, length us, event | category | flops | bytes accessed | tf_op | source)
XLA Modules:
  0.0 83.3 jit_solution(13809500321857743805)
XLA Ops:
  0.0 0.0 copy-start
  0.0 2.2 %copy-done = bf16[8192,256]{1,0:T(8,128)(2,1)S(1)} copy-done((bf16[8192,256]{1,0:T(8,128)(2,1)S(1)}, bf16[8192,256]{1,0:T(8,128)(2,1)}, u32[]{:S(2)}) %copy-start) | copy-done | bytes 4194328
  2.2 0.0 copy-start.1
  2.2 1.5 %copy-done.1 = bf16[896,1024]{1,0:T(8,128)(2,1)S(1)} copy-done((bf16[896,1024]{1,0:T(8,128)(2,1)S(1)}, bf16[896,1024]{1,0:T(8,128)(2,1)}, u32[]{:S(2)}) %copy-start.1) | copy-done | bytes 1835032
  3.7 0.0 copy-start.2
  3.7 1.0 %copy-done.2 = bf16[32,8192]{1,0:T(8,128)(2,1)S(1)} copy-done((bf16[32,8192]{1,0:T(8,128)(2,1)S(1)}, bf16[32,8192]{1,0:T(8,128)(2,1)}, u32[]{:S(2)}) %copy-start.2) | copy-done | bytes 524312
  4.7 0.0 copy-start.3
  4.7 0.8 copy-done.3
  5.6 0.0 copy-start.4
  5.6 0.7 copy-done.4
  6.2 76.1 %shard_map.55 = f32[1024,256]{1,0:T(8,128)S(1)} custom-call(bf16[32,896]{1,0:T(8,128)(2,1)S(1)} %copy-done.3, bf16[32,8192]{1,0:T(8,128)(2,1)S(1)} %copy-done.2, bf16[896,1024]{1,0:T(8,128)(2,1)S(1)} %copy-done.1, bf16[8192,256]{1,0:T(8,128)(2,1)S(1)} %copy-done, s32[2]{0:T(128)S(1)} %copy-done.4), custom_call_target="tpu_custom_call" | custom-call | flops 2300000000 | bytes 8000000 | tf_op jit(solution)/shard_map/pallas_call | solution.py:335
  82.3 1.0 %copy.7 = f32[1024,256]{1,0:T(8,128)} copy(f32[1024,256]{1,0:T(8,128)S(1)} %shard_map.55) | data formatting | bytes 2097152
Async XLA Ops:
  0.0 2.2 %copy-start = (bf16[8192,256]{1,0:T(8,128)(2,1)S(1)}, bf16[8192,256]{1,0:T(8,128)(2,1)}, u32[]{:S(2)}) copy-start(bf16[8192,256]{1,0:T(8,128)(2,1)} %wo_in.1) | copy-start | bytes 12582916
  2.2 1.5 %copy-start.1 = (bf16[896,1024]{1,0:T(8,128)(2,1)S(1)}, bf16[896,1024]{1,0:T(8,128)(2,1)}, u32[]{:S(2)}) copy-start(bf16[896,1024]{1,0:T(8,128)(2,1)} %wi_in.1) | copy-start | bytes 5505028
  3.7 1.0 %copy-start.2 = (bf16[32,8192]{1,0:T(8,128)(2,1)S(1)}, bf16[32,8192]{1,0:T(8,128)(2,1)}, u32[]{:S(2)}) copy-start(bf16[32,8192]{1,0:T(8,128)(2,1)} %grad_in.1) | copy-start | bytes 1572868
  4.7 0.8 copy-start.3
  5.6 0.7 copy-start.4

commit v2 on v1

--- a/solution.py
+++ b/solution.py
@@ -12,10 +12,19 @@
 
 NZ = 12
 NY = 8
-SIZES = (192, 256, 256, 64)
-OFFS = (0, 192, 448, 704)
+SIZES = (192, 128, 128, 128, 192)
+OFFS = tuple(sum(SIZES[:g]) for g in range(len(SIZES)))
 SLOT = 64
 HALF = 32
+SCHEDULE = [
+    ("z0",), ("wi",), ("grad1",), ("z", 0, 1), ("z", 2, 0), ("grad2",), ("z", 2, 1), ("mm", 1),
+    ("zw", 1), ("mm", 0), ("c", 1), ("c", 0), ("z", 4, 0), ("x", 1), ("z", 4, 1), ("zw", 3),
+    ("mm", 2), ("mm", 3), ("x", 0), ("c", 2), ("c", 3), ("y", 1), ("g", 0), ("zw", 6), ("zw", 5),
+    ("mm", 4), ("x", 2), ("c", 4), ("x", 3), ("y", 0), ("g", 2), ("f", 1), ("x", 4), ("y", 3),
+    ("gw", 3), ("f", 0), ("gw", 1), ("y", 2), ("y", 4), ("fx", 1), ("g", 4), ("fx", 0), ("f", 3),
+    ("f", 2), ("fx", 3), ("gw", 5), ("f", 4), ("gw", 6), ("fx", 2), ("docs",), ("fc", 3), ("fc", 0),
+    ("fc", 1), ("fc", 2), ("outer", 0), ("fx", 4), ("fc", 4), ("outer", 1),
+]
 
 
 def up(k):
@@ -28,7 +37,7 @@
 
 def kernel(
     act_in, grad_in, wi_in, wo_in, lengths, out,
-    act, grads, wi, wo, gall, gdoc, part, core_r, x_s, x_r, y_s, y_r, full,
+    act, grads, wi, wo, gall, gdoc, part, core_r, x_s, x_r, y_s, y_r, full, prod,
     local_sem, z_ss, z_rs, g_ss, g_rs, r_ss, r_rs,
 ):
     ein = lax.axis_index("ein")
@@ -39,8 +48,9 @@
     x_hi = lax.rem(eout, 2)
     z = lax.div(eout, 2)
 
-    z_up = (ein, lax.rem(z + 1, NZ) * 2 + x_hi)
-    z_dn = (ein, lax.rem(z + NZ - 1, NZ) * 2 + x_hi)
+    z_peer = {
+        ("u", n): (ein, lax.rem(z + NZ - n, NZ) * 2 + x_hi) for n in (1, 2)
+    } | {("d", n): (ein, lax.rem(z + n, NZ) * 2 + x_hi) for n in (1, 2)}
     hi_peer = (ein, z * 2 + 1 - x_hi)
     core_peer = (ein + 1 - 2 * core, eout)
     x_peer = (ein + 2 - 4 * x_lo, eout)
@@ -60,12 +70,13 @@
     wi_copy.start()
 
     barrier = pltpu.get_barrier_semaphore()
-    partners = [z_up, z_dn, hi_peer, core_peer, x_peer] + y_peer[1:]
+    partners = [*z_peer.values(), hi_peer, core_peer, x_peer, *y_peer[1:]]
     for peer in partners:
         pl.semaphore_signal(barrier, inc=1, device_id=peer, device_id_type=MESH)
     pl.semaphore_wait(barrier, len(partners))
 
     started = []
+    state = {}
 
     def send(src, dst, ss, rs, peer):
         copy = pltpu.make_async_remote_copy(
@@ -81,28 +92,34 @@
     def act_unit(slot, h):
         return act.at[pl.ds(slot * SLOT + h * HALF, HALF)]
 
-    def z_send(k, h):
-        if k < 6 and not (k == 5 and h == 1):
-            i = (k * 2 + h) * 2
-            z_in["u", k + 1, h] = send(
-                act_unit(up(k), h), act_unit(up(k + 1) if k < 5 else 11, h),
-                z_ss.at[i], z_rs.at[i], z_dn)
-        if k < 6 and not (k == 5 and h == 0):
-            i = (k * 2 + h) * 2 + 1
-            z_in["d", k + 1, h] = send(
-                act_unit(down(k), h), act_unit(down(k + 1), h),
-                z_ss.at[i], z_rs.at[i], z_up)
+    slot_of = {"u": up, "d": down}
+
+    def z_send(way, k, h, n):
+        if k + n == 6 and way != "ud"[h]:
+            return
+        i = (k + n) * 4 + h * 2 + "ud".index(way)
+        to = 11 if k + n == 6 else slot_of[way](k + n)
+        z_in[way, k + n, h] = send(
+            act_unit(slot_of[way](k), h), act_unit(to, h), z_ss.at[i], z_rs.at[i], z_peer[way, n])
 
     def z_serve(k, h):
+        if k == 0 and h == 1:
+            state["hi_act"].wait_recv()
+        for way in "ud":
+            if k > 0:
+                z_in[way, k, h].wait_recv()
+            z_send(way, k, h, 2)
+            if k > 0:
+                z_send(way, k, h, 1)
         if k == 0:
-            hi_act.wait_recv()
-            z_send(0, 1)
-            return
-        for way in "ud":
-            if (way, k, h) in z_in:
-                z_in[way, k, h].wait_recv()
-        if k < 6:
-            z_send(k, h)
+            for way in "ud":
+                z_send(way, k, h, 1)
+
+    def z_wait(k):
+        for h in range(2):
+            for way in "ud":
+                if (way, k, h) in z_in:
+                    z_in[way, k, h].wait_recv()
 
     g_in = {}
 
@@ -111,18 +128,25 @@
             return gall.at[pl.ds(slot * SLOT, SLOT)]
         return gall.at[pl.ds(slot * SLOT + h * HALF, HALF)]
 
+    def g_send(way, k, n):
+        i = (k + n) * 2 + "ud".index(way)
+        h = "ud".index(way) if k + n == 6 else None
+        to = 11 if k + n == 6 else slot_of[way](k + n)
+        g_in[way, k + n] = send(
+            g_rows(slot_of[way](k), h), g_rows(to, h), g_ss.at[i], g_rs.at[i], z_peer[way, n])
+
     def g_serve(k):
         if k == 0:
-            hi_grad.wait_recv()
-        else:
-            for way in "ud":
+            state["hi"].wait_recv()
+        for way in "ud":
+            if k > 0:
                 g_in[way, k].wait_recv()
-        if k < 5:
-            g_in["u", k + 1] = send(g_rows(up(k)), g_rows(up(k + 1)), g_ss.at[2 * k], g_rs.at[2 * k], z_dn)
-            g_in["d", k + 1] = send(g_rows(down(k)), g_rows(down(k + 1)), g_ss.at[2 * k + 1], g_rs.at[2 * k + 1], z_up)
-        elif k == 5:
-            g_in["u", 6] = send(g_rows(up(5), 0), g_rows(11, 0), g_ss.at[10], g_rs.at[10], z_dn)
-            g_in["d", 6] = send(g_rows(down(5), 1), g_rows(11, 1), g_ss.at[11], g_rs.at[11], z_up)
+            g_send(way, k, 2)
+            g_send(way, k, 1)
+
+    def g_wait(k):
+        for way in "ud":
+            g_in[way, k].wait_recv()
 
     def grad_part(first, count, total):
         def step(i, acc):
@@ -244,93 +268,67 @@
         wait_at(g, 17, 1 - core, x_lo, core_peer)
         wait_at(g, 18, 1 - core, 1 - x_lo, core_peer)
 
+    def grad_first():
+        grad_copy.wait()
+        for copy in wo_copies[:2]:
+            copy.wait()
+        state["total"] = grad_part(0, 4, jnp.zeros((HALF, 256), F32))
+
+    def grad_last():
+        for copy in wo_copies[2:]:
+            copy.wait()
+        grad_done(grad_part(4, 4, state["total"]))
+        state["hi"] = send(g_rows(0, 0), g_rows(0, 1), g_ss.at[0], g_rs.at[0], hi_peer)
+
+    def documents():
+        for slot in range(NZ):
+            k = (slot + 1) // 2
+            shift = k if slot % 2 else NZ - k
+            doc = lax.div(lax.rem(z + shift, NZ), NZ // 2)
+            rows = pl.ds(slot * SLOT, SLOT)
+            values = gall[rows, :]
+            zero = jnp.zeros_like(values)
+            gdoc[rows, 0:256] = jnp.where(doc == 0, values, zero)
+            gdoc[rows, 256:512] = jnp.where(doc == 1, values, zero)
+
+    def outer(last):
+        rows = pl.ds(OFFS[-1], SIZES[-1]) if last else pl.ds(0, OFFS[-1])
+        if last:
+            denominator = (lengths[0] + lengths[1]).astype(F32)
+
+        def step(b, carry):
+            both = lax.dot_general(
+                full[b, rows, :], gdoc[rows, :], (((0,), (0,)), ((), ())),
+                preferred_element_type=F32)
+            if last:
+                both = both + prod[b]
+                squares = both[:, :256] * both[:, :256] + both[:, 256:] * both[:, 256:]
+                out[pl.ds(pl.multiple_of(b * 128, 128), 128), :] = squares / denominator
+            else:
+                prod[b] = both
+            return carry
+
+        lax.fori_loop(0, NY, step, 0)
+
+    def z_first():
+        state["hi_act"] = send(act_unit(0, 0), act_unit(0, 1), z_ss.at[0], z_rs.at[0], hi_peer)
+        z_serve(0, 0)
+
+    steps = {
+        "z0": z_first, "z": z_serve, "wi": wi_copy.wait, "g": g_serve, "grad1": grad_first,
+        "grad2": grad_last, "mm": gemm, "c": stage_c, "x": stage_x, "y": stage_y, "f": stage_f,
+        "fx": stage_fx, "fc": stage_fc, "docs": documents, "outer": outer,
+        "zw": z_wait, "gw": g_wait,
+    }
     act_copy.wait()
-    z_send(0, 0)
-    hi_act = send(act_unit(0, 0), act_unit(0, 1), z_ss.at[24], z_rs.at[24], hi_peer)
-    grad_copy.wait()
-    for copy in wo_copies[:2]:
-        copy.wait()
-    total = grad_part(0, 4, jnp.zeros((HALF, 256), F32))
-    z_serve(0, 1)
-    for copy in wo_copies[2:]:
-        copy.wait()
-    grad_done(grad_part(4, 4, total))
-    hi_grad = send(g_rows(0, 0), g_rows(0, 1), g_ss.at[12], g_rs.at[12], hi_peer)
-    z_serve(1, 0)
-    wi_copy.wait()
-    z_serve(1, 1)
-    gemm(0)
-    z_serve(2, 0)
-    g_serve(0)
-    z_serve(2, 1)
-    stage_c(0)
-    z_serve(3, 0)
-    g_serve(1)
-    z_serve(3, 1)
-    gemm(1)
-    stage_x(0)
-    z_serve(4, 0)
-    stage_c(1)
-    g_serve(2)
-    z_serve(4, 1)
-    stage_y(0)
-    z_serve(5, 0)
-    stage_x(1)
-    g_serve(3)
-    z_serve(5, 1)
-    gemm(2)
-    g_serve(4)
-    stage_f(0)
-    z_serve(6, 0)
-    z_serve(6, 1)
-    gemm(3)
-    stage_c(2)
-    stage_c(3)
-    stage_y(1)
-    stage_fx(0)
-    g_serve(5)
-    stage_x(2)
-    stage_x(3)
-    stage_f(1)
-    g_serve(6)
-
-    for slot in range(NZ):
-        k = (slot + 1) // 2
-        shift = k if slot % 2 else NZ - k
-        doc = lax.div(lax.rem(z + shift, NZ), NZ // 2)
-        rows = pl.ds(slot * SLOT, SLOT)
-        values = gall[rows, :]
-        zero = jnp.zeros_like(values)
-        gdoc[rows, 0:256] = jnp.where(doc == 0, values, zero)
-        gdoc[rows, 256:512] = jnp.where(doc == 1, values, zero)
-
-    stage_fx(1)
-    stage_y(2)
-    stage_y(3)
-    stage_f(2)
-    stage_f(3)
-    stage_fx(2)
-    stage_fx(3)
-    for g in range(4):
-        stage_fc(g)
-
-    denominator = (lengths[0] + lengths[1]).astype(F32)
-
-    def outer(b, carry):
-        both = lax.dot_general(
-            full[b], gdoc[...], (((0,), (0,)), ((), ())), preferred_element_type=F32)
-        squares = both[:, :256] * both[:, :256] + both[:, 256:] * both[:, 256:]
-        out[pl.ds(pl.multiple_of(b * 128, 128), 128), :] = squares / denominator
-        return carry
-
-    lax.fori_loop(0, NY, outer, 0)
-
+    for name, *at in SCHEDULE:
+        steps[name](*at)
     for copy in started:
         copy.wait_send()
 
 
 def body(activations, gradients, eigvec_in, eigvec_out, lengths):
-    anywhere = pl.BlockSpec(memory_space=pl.ANY)
+    anywhere = pl.BlockSpec(memory_space=pltpu.HBM)
     dma = pltpu.SemaphoreType.DMA
     return pl.pallas_call(
         kernel,
@@ -351,16 +349,17 @@
             pltpu.VMEM((8, 192, 128), BF16),
             pltpu.VMEM((7, 192, 128), BF16),
             pltpu.VMEM((8, 768, 128), BF16),
+            pltpu.VMEM((8, 128, 512), F32),
             dma((7,)),
-            dma((25,)),
-            dma((25,)),
-            dma((13,)),
-            dma((13,)),
-            dma((76,)),
-            dma((76,)),
+            dma((28,)),
+            dma((28,)),
+            dma((14,)),
+            dma((14,)),
+            dma((19 * len(SIZES),)),
+            dma((19 * len(SIZES),)),
         ],
         compiler_params=pltpu.CompilerParams(
-            collective_id=0, has_side_effects=True, vmem_limit_bytes=40 * 1024 * 1024),
+            collective_id=0, has_side_effects=True, vmem_limit_bytes=60 * 1024 * 1024),
         cost_estimate=pl.CostEstimate(
             flops=2_300_000_000, bytes_accessed=8_000_000, transcendentals=0),
     )(activations, gradients, eigvec_in, eigvec_out, lengths)

time: 83.6 us -> 71.9 us (0.86)
  Pallas kernels: 76.1 us -> 69.5 us
  local copies, waits for them, and re-layouts: 7.17 us -> 2.26 us
    pallas_call x1, Pallas kernels: 76.1 us -> 69.5 us  [body(): pl.pallas_call(kernel, out_shape=jax.ShapeDtypeStruct((1024, 256), F32),...]
    unnamed x11 -> x1, local copies, waits for them, and re-layouts: 7.17 us -> 2.26 us
where the time goes in v2:
time: 71.9 us; the launch traced here: 71.7 us
  Pallas kernels  69.5 us (97%)
  local copies, waits for them, and re-layouts  2.26 us (3%)
    pallas_call x1, Pallas kernels, body(): pl.pallas_call(kernel, out_shape=jax.ShapeDtypeStruct((1024, 256), F32),...  69.5 us
    unnamed x1, local copies, waits for them, and re-layouts  2.26 us

profile of v2, /device:TPU:1, one launch (start us, length us, event | category | flops | bytes accessed | tf_op | source)
XLA Modules:
  0.0 71.7 jit_solution(16228764259212119581)
XLA Ops:
  0.0 69.5 %shard_map.55 = f32[1024,256]{1,0:T(8,128)} custom-call(bf16[32,896]{1,0:T(8,128)(2,1)} %act_in.1, bf16[32,8192]{1,0:T(8,128)(2,1)} %grad_in.1, bf16[896,1024]{1,0:T(8,128)(2,1)} %wi_in.1, bf16[8192,256]{1,0:T(8,128)(2,1)} %wo_in.1, s32[2]{0:T(128)} %lengths.1), custom_call_target="tpu_custom_call" | custom-call | flops 2300000000 | bytes 8000000 | tf_op jit(solution)/shard_map/pallas_call | solution.py:333
  69.5 2.3 %copy.7 = f32[1024,256]{1,0:T(8,128)} copy(f32[1024,256]{1,0:T(8,128)} %shard_map.55) | data formatting | bytes 2097152

commit v3 on v2

--- a/solution.py
+++ b/solution.py
@@ -332,7 +332,7 @@
     dma = pltpu.SemaphoreType.DMA
     return pl.pallas_call(
         kernel,
-        out_shape=jax.ShapeDtypeStruct((1024, 256), F32),
+        out_shape=pltpu.VMEM((1024, 256), F32),
         in_specs=[anywhere] * 4 + [pl.BlockSpec(memory_space=pltpu.SMEM)],
         out_specs=pl.BlockSpec(memory_space=pltpu.VMEM),
         scratch_shapes=[

time: 71.9 us -> 69.5 us (0.967)
  local copies, waits for them, and re-layouts: 2.26 us -> 0.97 us
  Pallas kernels: 69.5 us -> 68.4 us
    unnamed x1, local copies, waits for them, and re-layouts: 2.26 us -> 0.97 us
    pallas_call x1, Pallas kernels: 69.5 us -> 68.4 us  [body(): pl.pallas_call(kernel, out_shape=pltpu.VMEM((1024, 256), F32), in_specs=[...]
where the time goes in v3:
time: 69.5 us; the launch traced here: 69.4 us
  Pallas kernels  68.4 us (98%)
  local copies, waits for them, and re-layouts  0.97 us (1%)
    pallas_call x1, Pallas kernels, body(): pl.pallas_call(kernel, out_shape=pltpu.VMEM((1024, 256), F32), in_specs=[...  68.4 us

profile of v3, /device:TPU:1, one launch (start us, length us, event | category | flops | bytes accessed | tf_op | source)
XLA Modules:
  0.0 69.4 jit_solution(15606875386130601532)
XLA Ops:
  0.0 68.4 %shard_map.55 = f32[1024,256]{1,0:T(8,128)S(1)} custom-call(bf16[32,896]{1,0:T(8,128)(2,1)} %act_in.1, bf16[32,8192]{1,0:T(8,128)(2,1)} %grad_in.1, bf16[896,1024]{1,0:T(8,128)(2,1)} %wi_in.1, bf16[8192,256]{1,0:T(8,128)(2,1)} %wo_in.1, s32[2]{0:T(128)} %lengths.1), custom_call_target="tpu_custom_call" | custom-call | flops 2300000000 | bytes 8000000 | tf_op jit(solution)/shard_map/pallas_call | solution.py:333
  68.4 1.0 %copy.7 = f32[1024,256]{1,0:T(8,128)} copy(f32[1024,256]{1,0:T(8,128)S(1)} %shard_map.55) | data formatting | bytes 2097152

commit v4 on v3

--- a/solution.py
+++ b/solution.py
@@ -12,19 +12,8 @@
 
 NZ = 12
 NY = 8
-SIZES = (192, 128, 128, 128, 192)
-OFFS = tuple(sum(SIZES[:g]) for g in range(len(SIZES)))
 SLOT = 64
 HALF = 32
-SCHEDULE = [
-    ("z0",), ("wi",), ("grad1",), ("z", 0, 1), ("z", 2, 0), ("grad2",), ("z", 2, 1), ("mm", 1),
-    ("zw", 1), ("mm", 0), ("c", 1), ("c", 0), ("z", 4, 0), ("x", 1), ("z", 4, 1), ("zw", 3),
-    ("mm", 2), ("mm", 3), ("x", 0), ("c", 2), ("c", 3), ("y", 1), ("g", 0), ("zw", 6), ("zw", 5),
-    ("mm", 4), ("x", 2), ("c", 4), ("x", 3), ("y", 0), ("g", 2), ("f", 1), ("x", 4), ("y", 3),
-    ("gw", 3), ("f", 0), ("gw", 1), ("y", 2), ("y", 4), ("fx", 1), ("g", 4), ("fx", 0), ("f", 3),
-    ("f", 2), ("fx", 3), ("gw", 5), ("f", 4), ("gw", 6), ("fx", 2), ("docs",), ("fc", 3), ("fc", 0),
-    ("fc", 1), ("fc", 2), ("outer", 0), ("fx", 4), ("fc", 4), ("outer", 1),
-]
 
 
 def up(k):
@@ -33,6 +22,34 @@
 
 def down(k):
     return 2 * k if k < 6 else 11
+
+
+GROUPS = (
+    ((0, 0), (1, 0), (2, 0), (0, 1)),
+    ((1, 1), (2, 1)),
+    ((3, 0), (4, 0)),
+    ((3, 1), (4, 1)),
+    ((5, 0), (6, 0), (5, 1), (6, 1)),
+)
+ROW = {}
+OFFS = []
+for members in GROUPS:
+    OFFS.append(len(ROW) * HALF)
+    for k, h in members:
+        for slot in sorted({up(k), down(k)}):
+            ROW[slot, h] = len(ROW) * HALF
+SIZES = [end - start for start, end in zip(OFFS, OFFS[1:] + [NZ * SLOT])]
+
+SCHEDULE = [
+    ("z0",), ("z", 0, 1), ("grad1",), ("z", 2, 0), ("wi",), ("grad2",), ("zw", 1, 0), ("mm", 0),
+    ("c", 0), ("zw", 1, 1), ("z", 2, 1), ("mm", 1), ("z", 4, 0), ("c", 1), ("zw", 3, 0), ("mm", 2),
+    ("x", 0), ("c", 2), ("z", 4, 1), ("x", 1), ("zw", 3, 1), ("mm", 3), ("x", 2), ("c", 3),
+    ("y", 0), ("g", 0), ("zw", 6, 0), ("zw", 6, 1), ("zw", 5, 0), ("zw", 5, 1), ("mm", 4), ("y", 1),
+    ("c", 4), ("y", 2), ("g", 2), ("x", 3), ("f", 1), ("x", 4), ("f", 2), ("gw", 3), ("f", 0),
+    ("y", 3), ("g", 4), ("fx", 1), ("y", 4), ("f", 3), ("gw", 5), ("fx", 0), ("gw", 6), ("fx", 2),
+    ("f", 4), ("gw", 1), ("docs",), ("fc", 0), ("fx", 3), ("fc", 2), ("fc", 3), ("fc", 1),
+    ("outer", 0), ("fx", 4), ("fc", 4), ("outer", 1),
+]
 
 
 def kernel(
@@ -90,7 +107,7 @@
     z_in = {}
 
     def act_unit(slot, h):
-        return act.at[pl.ds(slot * SLOT + h * HALF, HALF)]
+        return act.at[pl.ds(ROW[slot, h], HALF)]
 
     slot_of = {"u": up, "d": down}
 
@@ -108,18 +125,18 @@
         for way in "ud":
             if k > 0:
                 z_in[way, k, h].wait_recv()
-            z_send(way, k, h, 2)
-            if k > 0:
+                z_send(way, k, h, 2)
                 z_send(way, k, h, 1)
+            else:
+                z_send(way, k, h, 2)
         if k == 0:
             for way in "ud":
                 z_send(way, k, h, 1)
 
-    def z_wait(k):
-        for h in range(2):
-            for way in "ud":
-                if (way, k, h) in z_in:
-                    z_in[way, k, h].wait_recv()
+    def z_wait(k, h):
+        for way in "ud":
+            if (way, k, h) in z_in:
+                z_in[way, k, h].wait_recv()
 
     g_in = {}
 
@@ -285,16 +302,17 @@
             k = (slot + 1) // 2
             shift = k if slot % 2 else NZ - k
             doc = lax.div(lax.rem(z + shift, NZ), NZ // 2)
-            rows = pl.ds(slot * SLOT, SLOT)
-            values = gall[rows, :]
-            zero = jnp.zeros_like(values)
-            gdoc[rows, 0:256] = jnp.where(doc == 0, values, zero)
-            gdoc[rows, 256:512] = jnp.where(doc == 1, values, zero)
+            for h in range(2):
+                rows = pl.ds(ROW[slot, h], HALF)
+                values = gall[pl.ds(slot * SLOT + h * HALF, HALF), :]
+                zero = jnp.zeros_like(values)
+                gdoc[rows, 0:256] = jnp.where(doc == 0, values, zero)
+                gdoc[rows, 256:512] = jnp.where(doc == 1, values, zero)
 
     def outer(last):
         rows = pl.ds(OFFS[-1], SIZES[-1]) if last else pl.ds(0, OFFS[-1])
         if last:
-            denominator = (lengths[0] + lengths[1]).astype(F32)
+            scale = 1.0 / jnp.full((1, 256), lengths[0] + lengths[1], jnp.int32).astype(F32)
 
         def step(b, carry):
             both = lax.dot_general(
@@ -303,7 +321,7 @@
             if last:
                 both = both + prod[b]
                 squares = both[:, :256] * both[:, :256] + both[:, 256:] * both[:, 256:]
-                out[pl.ds(pl.multiple_of(b * 128, 128), 128), :] = squares / denominator
+                out[pl.ds(pl.multiple_of(b * 128, 128), 128), :] = squares * scale
             else:
                 prod[b] = both
             return carry

time: 69.5 us -> 69.2 us (level)
  no operation moved by 1% of the time
where the time goes in v4:
time: 69.2 us; the launch traced here: 69.1 us
  Pallas kernels  68.1 us (98%)
  local copies, waits for them, and re-layouts  0.97 us (1%)
    pallas_call x1, Pallas kernels, body(): pl.pallas_call(kernel, out_shape=pltpu.VMEM((1024, 256), F32), in_specs=[...  68.1 us

profile of v4, /device:TPU:1, one launch (start us, length us, event | category | flops | bytes accessed | tf_op | source)
XLA Modules:
  0.0 69.1 jit_solution(13901605416507671808)
XLA Ops:
  0.0 68.1 %shard_map.55 = f32[1024,256]{1,0:T(8,128)S(1)} custom-call(bf16[32,896]{1,0:T(8,128)(2,1)} %act_in.1, bf16[32,8192]{1,0:T(8,128)(2,1)} %grad_in.1, bf16[896,1024]{1,0:T(8,128)(2,1)} %wi_in.1, bf16[8192,256]{1,0:T(8,128)(2,1)} %wo_in.1, s32[2]{0:T(128)} %lengths.1), custom_call_target="tpu_custom_call" | custom-call | flops 2300000000 | bytes 8000000 | tf_op jit(solution)/shard_map/pallas_call | solution.py:351
  68.1 1.0 %copy.7 = f32[1024,256]{1,0:T(8,128)} copy(f32[1024,256]{1,0:T(8,128)S(1)} %shard_map.55) | data formatting | bytes 2097152

commit v5 on v4

--- a/solution.py
+++ b/solution.py
@@ -74,6 +74,11 @@
     y_of = [lax.rem(y + d, NY) for d in range(NY)]
     y_peer = [(y_of[d] * 4 + x_lo * 2 + core, eout) for d in range(NY)]
 
+    barrier = pltpu.get_barrier_semaphore()
+    partners = [*z_peer.values(), hi_peer, core_peer, x_peer, *y_peer[1:]]
+    for peer in partners:
+        pl.semaphore_signal(barrier, inc=1, device_id=peer, device_id_type=MESH)
+
     act_copy = pltpu.make_async_copy(act_in, act.at[pl.ds(0, HALF)], local_sem.at[0])
     act_copy.start()
     grad_copy = pltpu.make_async_copy(grad_in, grads, local_sem.at[1])
@@ -86,10 +91,6 @@
     wi_copy = pltpu.make_async_copy(wi_in, wi, local_sem.at[6])
     wi_copy.start()
 
-    barrier = pltpu.get_barrier_semaphore()
-    partners = [*z_peer.values(), hi_peer, core_peer, x_peer, *y_peer[1:]]
-    for peer in partners:
-        pl.semaphore_signal(barrier, inc=1, device_id=peer, device_id_type=MESH)
     pl.semaphore_wait(barrier, len(partners))
 
     started = []
@@ -116,8 +117,9 @@
             return
         i = (k + n) * 4 + h * 2 + "ud".index(way)
         to = 11 if k + n == 6 else slot_of[way](k + n)
+        own = act_in if k == 0 and h == 0 else act_unit(slot_of[way](k), h)
         z_in[way, k + n, h] = send(
-            act_unit(slot_of[way](k), h), act_unit(to, h), z_ss.at[i], z_rs.at[i], z_peer[way, n])
+            own, act_unit(to, h), z_ss.at[i], z_rs.at[i], z_peer[way, n])
 
     def z_serve(k, h):
         if k == 0 and h == 1:
@@ -329,7 +331,7 @@
         lax.fori_loop(0, NY, step, 0)
 
     def z_first():
-        state["hi_act"] = send(act_unit(0, 0), act_unit(0, 1), z_ss.at[0], z_rs.at[0], hi_peer)
+        state["hi_act"] = send(act_in, act_unit(0, 1), z_ss.at[0], z_rs.at[0], hi_peer)
         z_serve(0, 0)
 
     steps = {
@@ -338,8 +340,9 @@
         "fx": stage_fx, "fc": stage_fc, "docs": documents, "outer": outer,
         "zw": z_wait, "gw": g_wait,
     }
-    act_copy.wait()
     for name, *at in SCHEDULE:
+        if name == "wi":
+            act_copy.wait()
         steps[name](*at)
     for copy in started:
         copy.wait_send()

time: 69.2 us -> 68.9 us (level)
  no operation moved by 1% of the time
where the time goes in v5:
time: 68.9 us; the launch traced here: 68.8 us
  Pallas kernels  67.8 us (98%)
  local copies, waits for them, and re-layouts  0.97 us (1%)
    pallas_call x1, Pallas kernels, body(): pl.pallas_call(kernel, out_shape=pltpu.VMEM((1024, 256), F32), in_specs=[...  67.8 us

profile of v5, /device:TPU:1, one launch (start us, length us, event | category | flops | bytes accessed | tf_op | source)
XLA Modules:
  0.0 68.8 jit_solution(16817400859619620451)
XLA Ops:
  0.0 67.8 %shard_map.55 = f32[1024,256]{1,0:T(8,128)S(1)} custom-call(bf16[32,896]{1,0:T(8,128)(2,1)} %act_in.1, bf16[32,8192]{1,0:T(8,128)(2,1)} %grad_in.1, bf16[896,1024]{1,0:T(8,128)(2,1)} %wi_in.1, bf16[8192,256]{1,0:T(8,128)(2,1)} %wo_in.1, s32[2]{0:T(128)} %lengths.1), custom_call_target="tpu_custom_call" | custom-call | flops 2300000000 | bytes 8000000 | tf_op jit(solution)/shard_map/pallas_call | solution.py:354
  67.8 1.0 %copy.7 = f32[1024,256]{1,0:T(8,128)} copy(f32[1024,256]{1,0:T(8,128)S(1)} %shard_map.55) | data formatting | bytes 2097152
